TPU v7x, 512 devices: a whole 4x8x8 slice. The times are simulated.
512 devices in a mesh: ctx: 64 (over x, z, core), tp: 8 (over y).
Axes of the slice: x: 4, y: 8, z: 8, core: 2. Of those that a mesh axis runs over, the one named last changes fastest.
Arguments:
- features: bfloat16 [128, 196, 1152], P('ctx', None, 'tp'), may hold values from -6 to 6
- group_kernel: bfloat16 [9, 1152, 48], P(None, 'tp'), may hold values from -0.3125 to 0.3125
- squeeze_in: bfloat16 [1152, 288], P('tp'), may hold values from -0.75 to 0.75
- squeeze_out: bfloat16 [288, 1152], P(None, 'tp'), may hold values from -0.75 to 0.75
- sampler_kernel: bfloat16 [1152, 8, 1152], P('ctx', None, 'tp'), may hold values from -0.0625 to 0.0625
- readout_kernel: bfloat16 [1152, 8192], P('ctx', 'tp'), may hold values from -0.1875 to 0.1875
- frame_clip: int32 [128], replicated, may hold values from 0 to 15, as said below
- clip_keep: int32 [16], replicated, may hold values from 1 to 512, as said below
- token_cotangent: bfloat16 [4096, 8192], P('ctx', 'tp'), may hold values from -6 to 6
Outputs:
- llm_tokens: bfloat16 [4096, 8192], P('ctx', 'tp')
- grad_features: bfloat16 [128, 196, 1152], P('ctx', None, 'tp')
Inputs may be any that keep to these rules, and one draw needn't show every extreme that they name: `frame_clip`: clip ids start at 0 and never fall along the frames; every clip covers an even number of frames from 2 to 16 and starts at an even frame; some clip covers 16. `clip_keep`: each clip keeps at least one and at most 8 * 8 times half its frames of its tokens; the clip of 16 frames keeps all of its tokens, and some clip keeps a single token.
All inputs are finite; a program needn't handle non-finite values.
Results may differ from a plain program's by a relative error of at most 0.009.
Values may be sent and summed in bfloat16 or wider, within the bound.
A program may use at most 64 MiB of HBM per device.

v0:
```python
import jax
import jax.numpy as jnp
from jax import lax
from jax.sharding import PartitionSpec as P

SIDE = 14
OUT_SIDE = 8


def shifted(value, axis, by):
    count = lax.axis_size(axis)
    pairs = [(i, i + by) for i in range(count) if 0 <= i + by < count]
    return lax.ppermute(value, axis, pairs)


def silu_slope(values):
    sigma = jax.nn.sigmoid(values)
    return sigma * (1.0 + values * (1.0 - sigma))


def grouped_forward(frames_grid, group_kernel):
    count, side, _, chans = frames_grid.shape
    width = group_kernel.shape[2]
    groups = chans // width
    padded = jnp.pad(frames_grid, ((0, 0), (1, 1), (1, 1), (0, 0)))
    kernel = group_kernel.reshape(9, groups, width, width)
    total = jnp.zeros((count, side, side, groups, width), jnp.float32)
    for kernel_tap in range(9):
        row_shift, col_shift = divmod(kernel_tap, 3)
        window = padded[:, row_shift : row_shift + side, col_shift : col_shift + side]
        window = window.reshape(count, side, side, groups, width)
        total = total + jnp.einsum(
            "fyxgi,gio->fyxgo", window, kernel[kernel_tap], preferred_element_type=jnp.float32
        )
    return total.reshape(count, side, side, chans)


def grouped_backward(grad_grid, group_kernel):
    count, side, _, chans = grad_grid.shape
    width = group_kernel.shape[2]
    groups = chans // width
    kernel = group_kernel.reshape(9, groups, width, width)
    source = grad_grid.reshape(count, side, side, groups, width)
    total = jnp.zeros((count, side + 2, side + 2, chans), jnp.float32)
    for kernel_tap in range(9):
        row_shift, col_shift = divmod(kernel_tap, 3)
        spread = jnp.einsum(
            "fyxgo,gio->fyxgi", source, kernel[kernel_tap], preferred_element_type=jnp.float32
        )
        spread = spread.reshape(count, side, side, chans)
        total = total + jnp.pad(
            spread, ((0, 0), (row_shift, 2 - row_shift), (col_shift, 2 - col_shift), (0, 0))
        )
    return total[:, 1 : side + 1, 1 : side + 1]


def make_patches(prev_odd, even):
    stacked = jnp.stack([prev_odd, even], axis=1)
    stacked = jnp.pad(stacked, ((0, 0), (0, 0), (1, 1), (1, 1), (0, 0)))
    pairs, _, padded_side, _, chans = stacked.shape
    half = padded_side // 2
    shaped = stacked.reshape(pairs, 2, half, 2, half, 2, chans).transpose(0, 2, 4, 1, 3, 5, 6)
    return shaped.reshape(pairs * half * half, 8 * chans)


def unpatch(grad_rows, pairs, side, chans):
    half = side // 2 + 1
    shaped = grad_rows.reshape(pairs, half, half, 2, 2, 2, chans).transpose(0, 3, 1, 4, 2, 5, 6)
    shaped = shaped.reshape(pairs, 2, 2 * half, 2 * half, chans)
    return shaped[:, :, 1 : side + 1, 1 : side + 1]


def contract_last(left, right):
    return lax.dot_general(
        left, right, (((1,), (1,)), ((), ())), preferred_element_type=jnp.float32
    )


def per_device(
    features,
    group_kernel,
    squeeze_in,
    squeeze_out,
    sampler_kernel,
    readout_kernel,
    frame_clip,
    clip_keep,
    token_cotangent,
):
    highest = lax.Precision.HIGHEST
    shard_index = lax.axis_index("ctx")
    frames_dev, cells, chans = features.shape
    pairs_dev = frames_dev // 2
    grid = features.reshape(frames_dev, SIDE, SIDE, chans)
    conv_out = grouped_forward(grid, group_kernel)
    active = jax.nn.silu(conv_out)
    pooled = jnp.mean(active, axis=(1, 2))
    squeezed = lax.psum(jnp.dot(pooled, squeeze_in.astype(jnp.float32), precision=highest), "tp")
    relaxed = jax.nn.silu(squeezed)
    excite = jax.nn.sigmoid(jnp.dot(relaxed, squeeze_out.astype(jnp.float32), precision=highest))
    hidden = (grid.astype(jnp.float32) + active * excite[:, None, None, :]).astype(jnp.bfloat16)
    full_sampler, full_readout = (
        lax.all_gather(sampler_kernel, "ctx", axis=0, tiled=True),
        lax.all_gather(readout_kernel, "ctx", axis=0, tiled=True),
    )
    sampler_rows = full_sampler.reshape(full_sampler.shape[0], 8 * chans)
    halo_frame = shifted(hidden[-1], "ctx", 1)
    local_clip = lax.dynamic_slice_in_dim(frame_clip, shard_index * frames_dev, frames_dev)
    edge_clip = lax.dynamic_slice_in_dim(
        frame_clip, jnp.maximum(shard_index * frames_dev - 1, 0), 1
    )
    first_keep = jnp.logical_and(shard_index > 0, edge_clip[0] == local_clip[0])
    later_keep = local_clip[1:-1:2] == local_clip[2::2]
    pair_mask = jnp.concatenate([first_keep[None], later_keep]).astype(jnp.float32)
    even = hidden[0::2]
    odd = hidden[1::2]
    prev_odd = jnp.concatenate([halo_frame[None], odd[:-1]], axis=0)
    prev_odd = prev_odd * pair_mask.astype(jnp.bfloat16)[:, None, None, None]
    patches = make_patches(prev_odd, even)
    per_frame = OUT_SIDE * OUT_SIDE
    pair_clip = frame_clip[0::2]
    clip_ids = jnp.arange(clip_keep.shape[0], dtype=jnp.int32)
    start_pair = jnp.sum((pair_clip[None, :] < clip_ids[:, None]).astype(jnp.int32), axis=1)
    own_clip = local_clip[0::2]
    one_hot = (own_clip[:, None] == clip_ids[None, :]).astype(jnp.int32)
    own_start = jnp.sum(one_hot * start_pair[None, :], axis=1)
    own_keep = jnp.sum(one_hot * clip_keep[None, :], axis=1)
    pair_index = shard_index * pairs_dev + jnp.arange(pairs_dev, dtype=jnp.int32)
    position = (pair_index - own_start)[:, None] * per_frame + jnp.arange(
        per_frame, dtype=jnp.int32
    )[None, :]
    live = (position < own_keep[:, None]).reshape(-1).astype(jnp.bfloat16)
    pre = lax.psum(contract_last(patches, sampler_rows), "tp")
    act = jax.nn.silu(pre).astype(jnp.bfloat16)
    tokens = (
        jnp.dot(act, full_readout, preferred_element_type=jnp.float32).astype(jnp.bfloat16)
        * live[:, None]
    )
    llm_tokens = lax.all_to_all(tokens, "ctx", split_axis=0, concat_axis=0, tiled=True)
    back = (
        lax.all_to_all(token_cotangent, "ctx", split_axis=0, concat_axis=0, tiled=True)
        * live[:, None]
    )
    grad_act = lax.psum(contract_last(back, full_readout), "tp")
    grad_pre = (grad_act * silu_slope(pre)).astype(jnp.bfloat16)
    grad_patches = jnp.dot(grad_pre, sampler_rows, preferred_element_type=jnp.float32)
    grad_taps = unpatch(grad_patches, pairs_dev, SIDE, chans)
    leading = grad_taps[:, 0] * pair_mask[:, None, None, None]
    incoming = shifted(leading[0].astype(jnp.bfloat16), "ctx", -1).astype(jnp.float32)
    grad_even = grad_taps[:, 1]
    grad_odd = jnp.concatenate([leading[1:], incoming[None]], axis=0)
    grad_hidden = jnp.stack([grad_even, grad_odd], axis=1).reshape(frames_dev, SIDE, SIDE, chans)
    grad_excite = jnp.sum(grad_hidden * active, axis=(1, 2))
    grad_inner = grad_excite * excite * (1.0 - excite)
    grad_relaxed = lax.psum(
        jnp.dot(grad_inner, squeeze_out.astype(jnp.float32).T, precision=highest), "tp"
    )
    grad_squeezed = grad_relaxed * silu_slope(squeezed)
    grad_pooled = jnp.dot(grad_squeezed, squeeze_in.astype(jnp.float32).T, precision=highest)
    grad_active = grad_hidden * excite[:, None, None, :] + grad_pooled[:, None, None, :] / cells
    grad_conv = (grad_active * silu_slope(conv_out)).astype(jnp.bfloat16)
    grad_grid = grad_hidden + grouped_backward(grad_conv, group_kernel)
    grad_features = grad_grid.astype(jnp.bfloat16).reshape(frames_dev, cells, chans)
    return (llm_tokens, grad_features)


def solution(mesh):
    placed = (
        P("ctx", None, "tp"),
        P(None, "tp", None),
        P("tp", None),
        P(None, "tp"),
        P("ctx", None, "tp"),
        P("ctx", "tp"),
        P(),
        P(),
        P("ctx", "tp"),
    )
    return jax.shard_map(
        per_device,
        mesh=mesh,
        in_specs=placed,
        out_specs=(P("ctx", "tp"), P("ctx", None, "tp")),
        check_vma=False,
    )
```

profile of v0, /device:TPU:6, one launch (start us, length us, event | category | flops | bytes accessed | tf_op | source)
XLA Modules:
  0.0 348.0 jit_solution(8308310035529797624)
XLA Ops:
  8.7 1.1 copy.230
  9.7 1.0 copy.240
  10.8 1.5 fusion.52
  12.4 2.3 pad_slice_fusion
  17.0 1.2 reshape.191
  18.2 0.8 copy.246
  19.0 2.0 reshape.192
  21.2 2.0 reshape.193
  27.1 17.6 %psum.28 = f32[2,288]{1,0:T(2,128)S(1)} all-reduce(f32[2,288]{1,0:T(2,128)S(1)} %fusion.54), channel_id=1, replica_groups=mesh['ctx'=64,'tp'=8] {'tp'}, use_global_device_ids=true, to_apply=%region_1.2 | all-reduce | flops 576 | bytes 4608 | tf_op jit(solution)/shard_map/psum | solution.py:98
  45.6 1.4 add_convert_fusion
  47.2 1.9 collective-permute-start
  51.1 15.2 %all-to-all-start.1 = ((bf16[64,2,512]{2,1,0:T(2,128)(2,1)}), bf16[64,2,512]{2,1,0:T(2,128)(2,1)S(1)}, u32[]{:S(2)}, u32[]{:S(2)}) async-start(bf16[64,2,512]{2,1,0:T(2,128)(2,1)} %reshape.225), calls=%async_computation.1 | async-start | bytes 262144 | tf_op jit(solution)/shard_map/all_to_all | solution.py:141
  71.6 0.9 reshape.196
  72.5 2.6 all-to-all-done.1
  75.3 24.2 %all-gather.6.cloned.1.call-done = bf16[64,18,1024]{2,1,0:T(8,128)(2,1)} async-done(((bf16[1,18,1024]{2,1,0:T(8,128)(2,1)}), bf16[64,18,1024]{2,1,0:T(8,128)(2,1)}) %all-gather.6.cloned.1.call-update) | async-done | bytes 2359312 | tf_op jit(solution)/shard_map/all_gather | solution.py:104
  99.5 2.9 reshape.212
  102.4 1.6 fusion.29
  104.0 81.3 %all-gather.4.cloned.1.call-done = bf16[1152,8,144]{2,1,0:T(8,128)(2,1)} async-done(((bf16[18,8,144]{2,1,0:T(8,128)(2,1)}), bf16[1152,8,144]{2,1,0:T(8,128)(2,1)}) %all-gather.4.cloned.1.call-update) | async-done | bytes 2654224 | tf_op jit(solution)/shard_map/all_gather | solution.py:103
  185.3 5.5 %copy.254 = bf16[1152,8,144]{0,2,1:T(8,128)(2,1)S(1)} copy(bf16[1152,8,144]{2,1,0:T(8,128)(2,1)} %all-gather.4.cloned.1.call-done) | data formatting | bytes 5308416 | tf_op jit(solution)/shard_map/all_gather | solution.py:103
  190.8 2.2 fusion.55
  193.1 77.1 %all-reduce.14.cloned.1.call-done = (f32[64,1152]{1,0:T(8,128)}, f32[64,1152]{1,0:T(8,128)}) async-done(((f32[64,1152]{1,0:T(8,128)}, f32[64,1152]{1,0:T(8,128)}), (f32[64,1152]{1,0:T(8,128)}, f32[64,1152]{1,0:T(8,128)})) %all-reduce.14.cloned.1.call-update) | async-done | bytes 589840 | tf_op jit(solution)/shard_map/psum | solution.py:144
  270.3 2.3 convolution_bitcast_fusion.14
  273.0 0.8 fusion.51
  273.8 2.1 collective-permute-start.1
  278.1 11.2 %all-to-all-start = ((bf16[64,2,512]{2,1,0:T(2,128)(2,1)}), bf16[64,2,512]{2,1,0:T(2,128)(2,1)S(1)}, u32[]{:S(2)}, u32[]{:S(2)}) async-start(bf16[64,2,512]{2,1,0:T(2,128)(2,1)} %reshape.227), calls=%async_computation | async-start | bytes 262144 | tf_op jit(solution)/shard_map/all_to_all | solution.py:139
  290.1 16.7 %psum.31 = f32[2,288]{1,0:T(2,128)S(1)} all-reduce(f32[2,288]{1,0:T(2,128)S(1)} %fusion.39), channel_id=1, replica_groups=mesh['ctx'=64,'tp'=8] {'tp'}, use_global_device_ids=true, to_apply=%region_8.9 | all-reduce | flops 576 | bytes 4608 | tf_op jit(solution)/shard_map/psum | solution.py:155
  308.1 1.1 convolution_bitcast_fusion.7
  309.2 1.1 convolution_bitcast_fusion.6
  310.3 1.1 convolution_bitcast_fusion.5
  311.4 1.1 convolution_bitcast_fusion.4
  312.6 1.1 convolution_bitcast_fusion.3
  314.8 1.3 reshape.201
  316.2 1.5 copy.264
  317.7 1.4 reshape.202
  319.0 1.5 copy.265
  320.5 1.4 reshape.203
  321.9 1.5 copy.266
  323.4 1.4 reshape.204
  324.8 1.5 copy.267
  326.3 1.4 reshape.205
  327.7 1.5 copy.268
  329.2 1.3 reshape.206
  330.9 1.4 reshape.207
  332.7 1.4 reshape.208
  334.5 1.4 reshape.209
  335.9 1.5 pad_add_fusion
  337.4 2.4 fusion.15
  339.8 0.8 copy.272
  (156 shorter events, 22.5 us)
Async XLA Ops:
  7.2 38.1 %copy-start = (bf16[288,144]{0,1:T(8,128)(2,1)S(1)}, bf16[288,144]{0,1:T(8,128)(2,1)}, u32[]{:S(2)}) copy-start(bf16[288,144]{0,1:T(8,128)(2,1)} %param.12) | copy-start | bytes 248836
  7.2 92.3 %all-gather.6.cloned.1.call-start = ((), (), s32[]{:S(2)}) async-start(), calls=%async_computation.3 | async-start | bytes 3194880 | tf_op jit(solution)/shard_map/all_gather | solution.py:104
  7.9 177.4 %all-gather.4.cloned.1.call-start = ((), (), s32[]{:S(2)}) async-start(), calls=%async_computation.2 | async-start | bytes 4792320 | tf_op jit(solution)/shard_map/all_gather | solution.py:103
  15.1 8.3 %copy-start.9 = (bf16[1,144,48]{2,1,0:T(8,128)(2,1)}, bf16[1,144,48]{2,1,0:T(8,128)(2,1)S(1)}, u32[]{:S(2)}) copy-start(bf16[1,144,48]{2,1,0:T(8,128)(2,1)S(1)} %copy.233) | copy-start | bytes 41476
  15.5 8.2 %copy-start.11 = (bf16[1,144,48]{2,1,0:T(8,128)(2,1)}, bf16[1,144,48]{2,1,0:T(8,128)(2,1)S(1)}, u32[]{:S(2)}) copy-start(bf16[1,144,48]{2,1,0:T(8,128)(2,1)S(1)} %copy.235) | copy-start | bytes 41476
  15.8 8.0 %copy-start.13 = (bf16[1,144,48]{2,1,0:T(8,128)(2,1)}, bf16[1,144,48]{2,1,0:T(8,128)(2,1)S(1)}, u32[]{:S(2)}) copy-start(bf16[1,144,48]{2,1,0:T(8,128)(2,1)S(1)} %copy.237) | copy-start | bytes 41476
  16.2 7.9 %copy-start.15 = (bf16[1,144,48]{2,1,0:T(8,128)(2,1)}, bf16[1,144,48]{2,1,0:T(8,128)(2,1)S(1)}, u32[]{:S(2)}) copy-start(bf16[1,144,48]{2,1,0:T(8,128)(2,1)S(1)} %copy.239) | copy-start | bytes 41476
  16.6 7.8 %copy-start.17 = (bf16[1,144,48]{2,1,0:T(8,128)(2,1)}, bf16[1,144,48]{2,1,0:T(8,128)(2,1)S(1)}, u32[]{:S(2)}) copy-start(bf16[1,144,48]{2,1,0:T(8,128)(2,1)S(1)} %copy.242) | copy-start | bytes 41476
  16.9 7.7 %copy-start.19 = (bf16[1,144,48]{2,1,0:T(8,128)(2,1)}, bf16[1,144,48]{2,1,0:T(8,128)(2,1)S(1)}, u32[]{:S(2)}) copy-start(bf16[1,144,48]{2,1,0:T(8,128)(2,1)S(1)} %copy.244) | copy-start | bytes 41476
  19.0 5.9 %copy-start.21 = (bf16[1,144,48]{2,1,0:T(8,128)(2,1)}, bf16[1,144,48]{2,1,0:T(8,128)(2,1)S(1)}, u32[]{:S(2)}) copy-start(bf16[1,144,48]{2,1,0:T(8,128)(2,1)S(1)} %copy.246) | copy-start | bytes 41476
  21.2 4.2 %copy-start.23 = (bf16[1,144,48]{2,1,0:T(8,128)(2,1)}, bf16[1,144,48]{2,1,0:T(8,128)(2,1)S(1)}, u32[]{:S(2)}) copy-start(bf16[1,144,48]{2,1,0:T(8,128)(2,1)S(1)} %copy.248) | copy-start | bytes 41476
  24.1 1.0 copy-start.7
  24.4 1.0 copy-start.8
  25.4 1.5 copy-start.26
  25.8 23.9 %copy-start.25 = (bf16[64,1024]{1,0:T(8,128)(2,1)S(1)}, bf16[64,1024]{1,0:T(8,128)(2,1)}, u32[]{:S(2)}) copy-start(bf16[64,1024]{1,0:T(8,128)(2,1)} %param.17) | copy-start | bytes 393220
  26.3 40.2 %copy-start.33 = (s32[128]{0:T(128)S(1)}, s32[128]{0:T(128)}, u32[]{:S(2)}) copy-start(s32[128]{0:T(128)} %param.15) | copy-start | bytes 1540
  26.3 43.2 %copy-start.34 = (s32[16]{0:T(128)S(1)}, s32[16]{0:T(128)}, u32[]{:S(2)}) copy-start(s32[16]{0:T(128)} %param.16) | copy-start | bytes 196
  44.7 0.6 copy-start.28
  47.2 23.6 %collective-permute-start = (bf16[14,14,144]{2,1,0:T(8,128)(2,1)S(1)}, bf16[14,14,144]{2,1,0:T(8,128)(2,1)S(1)}, u32[]{:S(2)}, u32[]{:S(2)}) collective-permute-start(bf16[14,14,144]{2,1,0:T(8,128)(2,1)S(1)} %bitcast.239), channel_id=1, source_target_pairs={{0,8},{8,16},{16,24},{24,32},{32,40},{40,48},{48,56},{56,64},{64,7... | collective-permute-start | bytes 169352 | tf_op jit(solution)/shard_map/ppermute | solution.py:13
  51.1 24.1 %all-to-all-start.1 = ((bf16[64,2,512]{2,1,0:T(2,128)(2,1)}), bf16[64,2,512]{2,1,0:T(2,128)(2,1)S(1)}, u32[]{:S(2)}, u32[]{:S(2)}) async-start(bf16[64,2,512]{2,1,0:T(2,128)(2,1)} %reshape.225), calls=%async_computation.1 | async-start | bytes 262144 | tf_op jit(solution)/shard_map/all_to_all | solution.py:141
  66.3 204.0 %all-reduce.14.cloned.1.call-start = ((), (), s32[]{:S(2)}) async-start(), calls=%async_computation.4 | async-start | bytes 1179648 | tf_op jit(solution)/shard_map/psum | solution.py:144
  70.8 31.6 %copy-start.30 = (bf16[64]{0:T(256)(128)(2,1)}, bf16[64]{0:T(256)(128)(2,1)S(1)}, u32[]{:S(2)}) copy-start(bf16[64]{0:T(256)(128)(2,1)S(1)} %compare_convert_fusion) | copy-start | bytes 388
  102.4 1.6 copy-start.1
  270.3 5.6 %copy-start.2 = (bf16[1152,1024]{1,0:T(8,128)(2,1)S(1)}, bf16[1152,1024]{1,0:T(8,128)(2,1)}, u32[]{:S(2)}) copy-start(bf16[1152,1024]{1,0:T(8,128)(2,1)} %copy-done.1) | copy-start | bytes 7077892
  270.3 5.6 %copy-start.31 = (bf16[64]{0:T(256)(128)(2,1)S(1)}, bf16[64]{0:T(256)(128)(2,1)}, u32[]{:S(2)}) copy-start(bf16[64]{0:T(256)(128)(2,1)} %copy-done.30) | copy-start | bytes 388
  270.3 5.6 %copy-start.32 = (f32[64,1152]{1,0:T(8,128)S(1)}, f32[64,1152]{1,0:T(8,128)}, u32[]{:S(2)}) copy-start(f32[64,1152]{1,0:T(8,128)} %get-tuple-element.15) | copy-start | bytes 884740
  273.8 15.7 %copy-start.3 = (f32[2,14,14,144]{3,0,2,1:T(2,128)S(1)}, f32[2,14,14,144]{3,0,2,1:T(2,128)}, u32[]{:S(2)}) copy-start(f32[2,14,14,144]{3,0,2,1:T(2,128)} %get-tuple-element.17) | copy-start | bytes 677380
  273.8 33.1 %copy-start.27 = (bf16[144,288]{1,0:T(8,128)(2,1)S(1)}, bf16[144,288]{1,0:T(8,128)(2,1)}, u32[]{:S(2)}) copy-start(bf16[144,288]{1,0:T(8,128)(2,1)} %param.11) | copy-start | bytes 248836
  273.8 33.1 %copy-start.29 = (f32[2,288]{1,0:T(2,128)S(1)}, f32[2,288]{1,0:T(2,128)}, u32[]{:S(2)}) copy-start(f32[2,288]{1,0:T(2,128)} %copy-done.28) | copy-start | bytes 6916
  273.8 15.5 %collective-permute-start.1 = (bf16[14,14,144]{2,1,0:T(8,128)(2,1)S(1)}, bf16[14,14,144]{2,1,0:T(8,128)(2,1)S(1)}, u32[]{:S(2)}, u32[]{:S(2)}) collective-permute-start(bf16[14,14,144]{2,1,0:T(8,128)(2,1)S(1)} %fusion.31), channel_id=1, source_target_pairs={{8,0},{16,8},{24,16},{32,24},{40,32},{48,40},{56,48},{64,56},{72,6... | collective-permute-start | bytes 169352 | tf_op jit(solution)/shard_map/ppermute | solution.py:13
  278.1 62.5 %all-to-all-start = ((bf16[64,2,512]{2,1,0:T(2,128)(2,1)}), bf16[64,2,512]{2,1,0:T(2,128)(2,1)S(1)}, u32[]{:S(2)}, u32[]{:S(2)}) async-start(bf16[64,2,512]{2,1,0:T(2,128)(2,1)} %reshape.227), calls=%async_computation | async-start | bytes 262144 | tf_op jit(solution)/shard_map/all_to_all | solution.py:139
  289.3 18.8 %copy-start.10 = (bf16[1,144,48]{2,1,0:T(8,128)(2,1)S(1)}, bf16[1,144,48]{2,1,0:T(8,128)(2,1)}, u32[]{:S(2)}) copy-start(bf16[1,144,48]{2,1,0:T(8,128)(2,1)} %copy-done.9) | copy-start | bytes 41476
  290.1 19.1 %copy-start.12 = (bf16[1,144,48]{2,1,0:T(8,128)(2,1)S(1)}, bf16[1,144,48]{2,1,0:T(8,128)(2,1)}, u32[]{:S(2)}) copy-start(bf16[1,144,48]{2,1,0:T(8,128)(2,1)} %copy-done.11) | copy-start | bytes 41476
  307.5 2.9 copy-start.14
  307.5 3.9 %copy-start.16 = (bf16[1,144,48]{2,1,0:T(8,128)(2,1)S(1)}, bf16[1,144,48]{2,1,0:T(8,128)(2,1)}, u32[]{:S(2)}) copy-start(bf16[1,144,48]{2,1,0:T(8,128)(2,1)} %copy-done.15) | copy-start | bytes 41476
  307.9 4.7 %copy-start.18 = (bf16[1,144,48]{2,1,0:T(8,128)(2,1)S(1)}, bf16[1,144,48]{2,1,0:T(8,128)(2,1)}, u32[]{:S(2)}) copy-start(bf16[1,144,48]{2,1,0:T(8,128)(2,1)} %copy-done.17) | copy-start | bytes 41476
  308.1 5.5 %copy-start.20 = (bf16[1,144,48]{2,1,0:T(8,128)(2,1)S(1)}, bf16[1,144,48]{2,1,0:T(8,128)(2,1)}, u32[]{:S(2)}) copy-start(bf16[1,144,48]{2,1,0:T(8,128)(2,1)} %copy-done.19) | copy-start | bytes 41476
  309.2 4.7 %copy-start.22 = (bf16[1,144,48]{2,1,0:T(8,128)(2,1)S(1)}, bf16[1,144,48]{2,1,0:T(8,128)(2,1)}, u32[]{:S(2)}) copy-start(bf16[1,144,48]{2,1,0:T(8,128)(2,1)} %copy-done.21) | copy-start | bytes 41476
  310.3 3.8 %copy-start.24 = (bf16[1,144,48]{2,1,0:T(8,128)(2,1)S(1)}, bf16[1,144,48]{2,1,0:T(8,128)(2,1)}, u32[]{:S(2)}) copy-start(bf16[1,144,48]{2,1,0:T(8,128)(2,1)} %copy-done.23) | copy-start | bytes 41476
  332.3 3.6 %copy-start.4 = (f32[2,14,14,144]{3,0,2,1:T(2,128)S(1)}, f32[2,14,14,144]{3,0,2,1:T(2,128)}, u32[]{:S(2)}) copy-start(f32[2,14,14,144]{3,0,2,1:T(2,128)} %reshape.201) | copy-start | bytes 677380
  334.1 3.3 copy-start.5
  334.5 2.9 copy-start.6
Sparse Core Ops, SparseCore 0:
  11.3 88.0 all-gather.5
  102.8 82.4 all-gather.3
  193.2 77.0 all-reduce.13
where the time goes:
time: 349 us; the launch traced here: 348 us
  waiting for transfers between devices  187 us (54%)
  local copies, waits for them, and re-layouts  54.8 us (16%)
  blocking collectives  34.3 us (10%)
  starting transfers between devices  30.7 us (9%)
  matrix products  16 us (5%)
  between operations  15.9 us (5%)
  other arithmetic  9.59 us (3%)
    all_gather x1, waiting for transfers between devices, per_device(): lax.all_gather(sampler_kernel, 'ctx', axis=0, tiled=True)  81.3 us
    psum x1, waiting for transfers between devices, per_device(): grad_act = lax.psum(contract_last(back, full_readout), 'tp')  77.1 us
    all_gather x1, waiting for transfers between devices, per_device(): lax.all_gather(readout_kernel, 'ctx', axis=0, tiled=True)  24.2 us
    psum x1, blocking collectives, per_device(): lax.psum(jnp.dot(pooled, squeeze_in.astype(jnp.float32), precision=highes...  17.6 us
    psum x1, blocking collectives, per_device(): lax.psum(jnp.dot(grad_inner, squeeze_out.astype(jnp.float32).T, precision...  16.7 us
    all_to_all x1, starting transfers between devices, per_device(): lax.all_to_all(token_cotangent, 'ctx', split_axis=0, concat_axis=0, tiled...  15.2 us
    reshape x9, local copies, waits for them, and re-layouts, grouped_backward(): spread = spread.reshape(count, side, side, chans)  12.2 us
    all_to_all x1, starting transfers between devices, per_device(): lax.all_to_all(tokens, 'ctx', split_axis=0, concat_axis=0, tiled=True)  11.2 us
  transfers between devices with their start and end apart: 7, of which 4 were waited for; matrix products, arithmetic and copies ran while one was open for 19% of the time, Pallas kernels for 0%

commit v1 on v0

--- a/solution.py
+++ b/solution.py
@@ -152,8 +152,11 @@
     grad_hidden = jnp.stack([grad_even, grad_odd], axis=1).reshape(frames_dev, SIDE, SIDE, chans)
     grad_excite = jnp.sum(grad_hidden * active, axis=(1, 2))
     grad_inner = grad_excite * excite * (1.0 - excite)
-    grad_relaxed = lax.psum(
-        jnp.dot(grad_inner, squeeze_out.astype(jnp.float32).T, precision=highest), "tp"
+    grad_relaxed = jnp.sum(
+        lax.all_gather(
+            jnp.dot(grad_inner, squeeze_out.astype(jnp.float32).T, precision=highest), "tp"
+        ),
+        axis=0,
     )
     grad_squeezed = grad_relaxed * silu_slope(squeezed)
     grad_pooled = jnp.dot(grad_squeezed, squeeze_in.astype(jnp.float32).T, precision=highest)

time: 349 us -> 357 us (1.023)
  blocking collectives: 34.3 us -> 42.3 us
    all_gather x0 -> x1, blocking collectives: none -> 24.7 us  [per_device(): lax.all_gather(jnp.dot(grad_inner, squeeze_out.astype(jnp.float32).T, pre...]
    psum x1 -> x0, blocking collectives: 16.7 us -> none  [per_device(): lax.psum(jnp.dot(grad_inner, squeeze_out.astype(jnp.float32).T, precision...]
where the time goes in v1:
time: 357 us; the launch traced here: 356 us
  waiting for transfers between devices  187 us (52%)
  local copies, waits for them, and re-layouts  54.8 us (15%)
  blocking collectives  42.3 us (12%)
  starting transfers between devices  30.7 us (9%)
  matrix products  16 us (4%)
  between operations  15.9 us (4%)
  other arithmetic  9.61 us (3%)
    all_gather x1, waiting for transfers between devices, per_device(): lax.all_gather(sampler_kernel, 'ctx', axis=0, tiled=True)  81.3 us
    psum x1, waiting for transfers between devices, per_device(): grad_act = lax.psum(contract_last(back, full_readout), 'tp')  77.1 us
    all_gather x1, blocking collectives, per_device(): lax.all_gather(jnp.dot(grad_inner, squeeze_out.astype(jnp.float32).T, pre...  24.7 us
    all_gather x1, waiting for transfers between devices, per_device(): lax.all_gather(readout_kernel, 'ctx', axis=0, tiled=True)  24.2 us
    psum x1, blocking collectives, per_device(): lax.psum(jnp.dot(pooled, squeeze_in.astype(jnp.float32), precision=highes...  17.6 us
    all_to_all x1, starting transfers between devices, per_device(): lax.all_to_all(token_cotangent, 'ctx', split_axis=0, concat_axis=0, tiled...  15.2 us
    reshape x9, local copies, waits for them, and re-layouts, grouped_backward(): spread = spread.reshape(count, side, side, chans)  12.2 us
    all_to_all x1, starting transfers between devices, per_device(): lax.all_to_all(tokens, 'ctx', split_axis=0, concat_axis=0, tiled=True)  11.2 us
  transfers between devices with their start and end apart: 7, of which 4 were waited for; matrix products, arithmetic and copies ran while one was open for 19% of the time, Pallas kernels for 0%

profile of v1, /device:TPU:6, one launch (start us, length us, event | category | flops | bytes accessed | tf_op | source)
XLA Modules:
  0.0 356.0 jit_solution(13159510728710075789)
XLA Ops:
  8.7 1.1 copy.230
  9.7 1.0 copy.240
  10.8 1.5 fusion.51
  12.4 2.3 pad_slice_fusion
  17.0 1.2 reshape.191
  18.2 0.8 copy.246
  19.0 2.0 reshape.192
  21.2 2.0 reshape.193
  27.1 17.6 %psum.21 = f32[2,288]{1,0:T(2,128)S(1)} all-reduce(f32[2,288]{1,0:T(2,128)S(1)} %fusion.53), channel_id=1, replica_groups=mesh['ctx'=64,'tp'=8] {'tp'}, use_global_device_ids=true, to_apply=%region_1.2 | all-reduce | flops 576 | bytes 4608 | tf_op jit(solution)/shard_map/psum | solution.py:98
  45.6 1.4 add_convert_fusion
  47.2 1.9 collective-permute-start
  51.1 15.2 %all-to-all-start.1 = ((bf16[64,2,512]{2,1,0:T(2,128)(2,1)}), bf16[64,2,512]{2,1,0:T(2,128)(2,1)S(1)}, u32[]{:S(2)}, u32[]{:S(2)}) async-start(bf16[64,2,512]{2,1,0:T(2,128)(2,1)} %reshape.229), calls=%async_computation.1 | async-start | bytes 262144 | tf_op jit(solution)/shard_map/all_to_all | solution.py:141
  71.6 0.9 reshape.196
  72.5 2.6 all-to-all-done.1
  75.3 24.2 %all-gather.8.cloned.1.call-done = bf16[64,18,1024]{2,1,0:T(8,128)(2,1)} async-done(((bf16[1,18,1024]{2,1,0:T(8,128)(2,1)}), bf16[64,18,1024]{2,1,0:T(8,128)(2,1)}) %all-gather.8.cloned.1.call-update) | async-done | bytes 2359312 | tf_op jit(solution)/shard_map/all_gather | solution.py:104
  99.5 2.9 reshape.213
  102.4 1.6 fusion.29
  104.0 81.3 %all-gather.6.cloned.1.call-done = bf16[1152,8,144]{2,1,0:T(8,128)(2,1)} async-done(((bf16[18,8,144]{2,1,0:T(8,128)(2,1)}), bf16[1152,8,144]{2,1,0:T(8,128)(2,1)}) %all-gather.6.cloned.1.call-update) | async-done | bytes 2654224 | tf_op jit(solution)/shard_map/all_gather | solution.py:103
  185.3 5.5 %copy.254 = bf16[1152,8,144]{0,2,1:T(8,128)(2,1)S(1)} copy(bf16[1152,8,144]{2,1,0:T(8,128)(2,1)} %all-gather.6.cloned.1.call-done) | data formatting | bytes 5308416 | tf_op jit(solution)/shard_map/all_gather | solution.py:103
  190.8 2.2 fusion.54
  193.1 77.1 %all-reduce.14.cloned.1.call-done = (f32[64,1152]{1,0:T(8,128)}, f32[64,1152]{1,0:T(8,128)}) async-done(((f32[64,1152]{1,0:T(8,128)}, f32[64,1152]{1,0:T(8,128)}), (f32[64,1152]{1,0:T(8,128)}, f32[64,1152]{1,0:T(8,128)})) %all-reduce.14.cloned.1.call-update) | async-done | bytes 589840 | tf_op jit(solution)/shard_map/psum | solution.py:144
  270.3 2.3 convolution_bitcast_fusion.14
  273.0 0.8 fusion.50
  273.8 2.1 collective-permute-start.1
  278.1 11.2 %all-to-all-start = ((bf16[64,2,512]{2,1,0:T(2,128)(2,1)}), bf16[64,2,512]{2,1,0:T(2,128)(2,1)S(1)}, u32[]{:S(2)}, u32[]{:S(2)}) async-start(bf16[64,2,512]{2,1,0:T(2,128)(2,1)} %reshape.231), calls=%async_computation | async-start | bytes 262144 | tf_op jit(solution)/shard_map/all_to_all | solution.py:139
  290.1 24.7 %all-gather.2 = f32[8,2,288]{2,1,0:T(2,128)S(1)} all-gather(f32[1,2,288]{2,1,0:T(2,128)S(1)} %convolution_bitcast_fusion.15), channel_id=2, replica_groups=mesh['ctx'=64,'tp'=8] {'tp'}, dimensions={0}, use_global_device_ids=true | all-gather | bytes 20736 | tf_op jit(solution)/shard_map/all_gather | solution.py:156
  316.1 1.1 convolution_bitcast_fusion.7
  317.2 1.1 convolution_bitcast_fusion.6
  318.3 1.1 convolution_bitcast_fusion.5
  319.4 1.1 convolution_bitcast_fusion.4
  320.6 1.1 convolution_bitcast_fusion.3
  322.8 1.3 reshape.201
  324.2 1.5 copy.264
  325.7 1.4 reshape.202
  327.0 1.5 copy.265
  328.5 1.4 reshape.203
  329.9 1.5 copy.266
  331.4 1.4 reshape.204
  332.8 1.5 copy.267
  334.3 1.4 reshape.205
  335.7 1.5 copy.268
  337.2 1.3 reshape.206
  338.9 1.4 reshape.207
  340.7 1.4 reshape.208
  342.5 1.4 reshape.209
  343.9 1.5 pad_add_fusion
  345.4 2.4 fusion.15
  347.8 0.8 copy.272
  (157 shorter events, 22.5 us)
Async XLA Ops:
  7.2 38.1 %copy-start = (bf16[288,144]{0,1:T(8,128)(2,1)S(1)}, bf16[288,144]{0,1:T(8,128)(2,1)}, u32[]{:S(2)}) copy-start(bf16[288,144]{0,1:T(8,128)(2,1)} %param.12) | copy-start | bytes 248836
  7.2 92.3 %all-gather.8.cloned.1.call-start = ((), (), s32[]{:S(2)}) async-start(), calls=%async_computation.3 | async-start | bytes 3194880 | tf_op jit(solution)/shard_map/all_gather | solution.py:104
  7.9 177.4 %all-gather.6.cloned.1.call-start = ((), (), s32[]{:S(2)}) async-start(), calls=%async_computation.2 | async-start | bytes 4792320 | tf_op jit(solution)/shard_map/all_gather | solution.py:103
  15.1 8.3 %copy-start.9 = (bf16[1,144,48]{2,1,0:T(8,128)(2,1)}, bf16[1,144,48]{2,1,0:T(8,128)(2,1)S(1)}, u32[]{:S(2)}) copy-start(bf16[1,144,48]{2,1,0:T(8,128)(2,1)S(1)} %copy.233) | copy-start | bytes 41476
  15.5 8.2 %copy-start.11 = (bf16[1,144,48]{2,1,0:T(8,128)(2,1)}, bf16[1,144,48]{2,1,0:T(8,128)(2,1)S(1)}, u32[]{:S(2)}) copy-start(bf16[1,144,48]{2,1,0:T(8,128)(2,1)S(1)} %copy.235) | copy-start | bytes 41476
  15.8 8.0 %copy-start.13 = (bf16[1,144,48]{2,1,0:T(8,128)(2,1)}, bf16[1,144,48]{2,1,0:T(8,128)(2,1)S(1)}, u32[]{:S(2)}) copy-start(bf16[1,144,48]{2,1,0:T(8,128)(2,1)S(1)} %copy.237) | copy-start | bytes 41476
  16.2 7.9 %copy-start.15 = (bf16[1,144,48]{2,1,0:T(8,128)(2,1)}, bf16[1,144,48]{2,1,0:T(8,128)(2,1)S(1)}, u32[]{:S(2)}) copy-start(bf16[1,144,48]{2,1,0:T(8,128)(2,1)S(1)} %copy.239) | copy-start | bytes 41476
  16.6 7.8 %copy-start.17 = (bf16[1,144,48]{2,1,0:T(8,128)(2,1)}, bf16[1,144,48]{2,1,0:T(8,128)(2,1)S(1)}, u32[]{:S(2)}) copy-start(bf16[1,144,48]{2,1,0:T(8,128)(2,1)S(1)} %copy.242) | copy-start | bytes 41476
  16.9 7.7 %copy-start.19 = (bf16[1,144,48]{2,1,0:T(8,128)(2,1)}, bf16[1,144,48]{2,1,0:T(8,128)(2,1)S(1)}, u32[]{:S(2)}) copy-start(bf16[1,144,48]{2,1,0:T(8,128)(2,1)S(1)} %copy.244) | copy-start | bytes 41476
  19.0 5.9 %copy-start.21 = (bf16[1,144,48]{2,1,0:T(8,128)(2,1)}, bf16[1,144,48]{2,1,0:T(8,128)(2,1)S(1)}, u32[]{:S(2)}) copy-start(bf16[1,144,48]{2,1,0:T(8,128)(2,1)S(1)} %copy.246) | copy-start | bytes 41476
  21.2 4.2 %copy-start.23 = (bf16[1,144,48]{2,1,0:T(8,128)(2,1)}, bf16[1,144,48]{2,1,0:T(8,128)(2,1)S(1)}, u32[]{:S(2)}) copy-start(bf16[1,144,48]{2,1,0:T(8,128)(2,1)S(1)} %copy.248) | copy-start | bytes 41476
  24.1 1.0 copy-start.7
  24.4 1.0 copy-start.8
  25.4 1.5 copy-start.26
  25.8 23.9 %copy-start.25 = (bf16[64,1024]{1,0:T(8,128)(2,1)S(1)}, bf16[64,1024]{1,0:T(8,128)(2,1)}, u32[]{:S(2)}) copy-start(bf16[64,1024]{1,0:T(8,128)(2,1)} %param.17) | copy-start | bytes 393220
  26.3 40.2 %copy-start.33 = (s32[128]{0:T(128)S(1)}, s32[128]{0:T(128)}, u32[]{:S(2)}) copy-start(s32[128]{0:T(128)} %param.15) | copy-start | bytes 1540
  26.3 43.2 %copy-start.34 = (s32[16]{0:T(128)S(1)}, s32[16]{0:T(128)}, u32[]{:S(2)}) copy-start(s32[16]{0:T(128)} %param.16) | copy-start | bytes 196
  44.7 0.6 copy-start.28
  47.2 23.6 %collective-permute-start = (bf16[14,14,144]{2,1,0:T(8,128)(2,1)S(1)}, bf16[14,14,144]{2,1,0:T(8,128)(2,1)S(1)}, u32[]{:S(2)}, u32[]{:S(2)}) collective-permute-start(bf16[14,14,144]{2,1,0:T(8,128)(2,1)S(1)} %bitcast.241), channel_id=1, source_target_pairs={{0,8},{8,16},{16,24},{24,32},{32,40},{40,48},{48,56},{56,64},{64,7... | collective-permute-start | bytes 169352 | tf_op jit(solution)/shard_map/ppermute | solution.py:13
  51.1 24.1 %all-to-all-start.1 = ((bf16[64,2,512]{2,1,0:T(2,128)(2,1)}), bf16[64,2,512]{2,1,0:T(2,128)(2,1)S(1)}, u32[]{:S(2)}, u32[]{:S(2)}) async-start(bf16[64,2,512]{2,1,0:T(2,128)(2,1)} %reshape.229), calls=%async_computation.1 | async-start | bytes 262144 | tf_op jit(solution)/shard_map/all_to_all | solution.py:141
  66.3 204.0 %all-reduce.14.cloned.1.call-start = ((), (), s32[]{:S(2)}) async-start(), calls=%async_computation.4 | async-start | bytes 1179648 | tf_op jit(solution)/shard_map/psum | solution.py:144
  70.8 31.6 %copy-start.30 = (bf16[64]{0:T(256)(128)(2,1)}, bf16[64]{0:T(256)(128)(2,1)S(1)}, u32[]{:S(2)}) copy-start(bf16[64]{0:T(256)(128)(2,1)S(1)} %compare_convert_fusion) | copy-start | bytes 388
  102.4 1.6 copy-start.1
  270.3 5.6 %copy-start.2 = (bf16[1152,1024]{1,0:T(8,128)(2,1)S(1)}, bf16[1152,1024]{1,0:T(8,128)(2,1)}, u32[]{:S(2)}) copy-start(bf16[1152,1024]{1,0:T(8,128)(2,1)} %copy-done.1) | copy-start | bytes 7077892
  270.3 5.6 %copy-start.31 = (bf16[64]{0:T(256)(128)(2,1)S(1)}, bf16[64]{0:T(256)(128)(2,1)}, u32[]{:S(2)}) copy-start(bf16[64]{0:T(256)(128)(2,1)} %copy-done.30) | copy-start | bytes 388
  270.3 5.6 %copy-start.32 = (f32[64,1152]{1,0:T(8,128)S(1)}, f32[64,1152]{1,0:T(8,128)}, u32[]{:S(2)}) copy-start(f32[64,1152]{1,0:T(8,128)} %get-tuple-element.15) | copy-start | bytes 884740
  273.8 15.7 %copy-start.3 = (f32[2,14,14,144]{3,0,2,1:T(2,128)S(1)}, f32[2,14,14,144]{3,0,2,1:T(2,128)}, u32[]{:S(2)}) copy-start(f32[2,14,14,144]{3,0,2,1:T(2,128)} %get-tuple-element.17) | copy-start | bytes 677380
  273.8 41.1 %copy-start.27 = (bf16[144,288]{1,0:T(8,128)(2,1)S(1)}, bf16[144,288]{1,0:T(8,128)(2,1)}, u32[]{:S(2)}) copy-start(bf16[144,288]{1,0:T(8,128)(2,1)} %param.11) | copy-start | bytes 248836
  273.8 41.1 %copy-start.29 = (f32[2,288]{1,0:T(2,128)S(1)}, f32[2,288]{1,0:T(2,128)}, u32[]{:S(2)}) copy-start(f32[2,288]{1,0:T(2,128)} %copy-done.28) | copy-start | bytes 6916
  273.8 15.5 %collective-permute-start.1 = (bf16[14,14,144]{2,1,0:T(8,128)(2,1)S(1)}, bf16[14,14,144]{2,1,0:T(8,128)(2,1)S(1)}, u32[]{:S(2)}, u32[]{:S(2)}) collective-permute-start(bf16[14,14,144]{2,1,0:T(8,128)(2,1)S(1)} %fusion.31), channel_id=1, source_target_pairs={{8,0},{16,8},{24,16},{32,24},{40,32},{48,40},{56,48},{64,56},{72,6... | collective-permute-start | bytes 169352 | tf_op jit(solution)/shard_map/ppermute | solution.py:13
  278.1 70.5 %all-to-all-start = ((bf16[64,2,512]{2,1,0:T(2,128)(2,1)}), bf16[64,2,512]{2,1,0:T(2,128)(2,1)S(1)}, u32[]{:S(2)}, u32[]{:S(2)}) async-start(bf16[64,2,512]{2,1,0:T(2,128)(2,1)} %reshape.231), calls=%async_computation | async-start | bytes 262144 | tf_op jit(solution)/shard_map/all_to_all | solution.py:139
  289.4 26.7 %copy-start.10 = (bf16[1,144,48]{2,1,0:T(8,128)(2,1)S(1)}, bf16[1,144,48]{2,1,0:T(8,128)(2,1)}, u32[]{:S(2)}) copy-start(bf16[1,144,48]{2,1,0:T(8,128)(2,1)} %copy-done.9) | copy-start | bytes 41476
  290.1 27.1 %copy-start.12 = (bf16[1,144,48]{2,1,0:T(8,128)(2,1)S(1)}, bf16[1,144,48]{2,1,0:T(8,128)(2,1)}, u32[]{:S(2)}) copy-start(bf16[1,144,48]{2,1,0:T(8,128)(2,1)} %copy-done.11) | copy-start | bytes 41476
  315.5 2.9 copy-start.14
  315.5 3.9 %copy-start.16 = (bf16[1,144,48]{2,1,0:T(8,128)(2,1)S(1)}, bf16[1,144,48]{2,1,0:T(8,128)(2,1)}, u32[]{:S(2)}) copy-start(bf16[1,144,48]{2,1,0:T(8,128)(2,1)} %copy-done.15) | copy-start | bytes 41476
  315.8 4.7 %copy-start.18 = (bf16[1,144,48]{2,1,0:T(8,128)(2,1)S(1)}, bf16[1,144,48]{2,1,0:T(8,128)(2,1)}, u32[]{:S(2)}) copy-start(bf16[1,144,48]{2,1,0:T(8,128)(2,1)} %copy-done.17) | copy-start | bytes 41476
  316.1 5.5 %copy-start.20 = (bf16[1,144,48]{2,1,0:T(8,128)(2,1)S(1)}, bf16[1,144,48]{2,1,0:T(8,128)(2,1)}, u32[]{:S(2)}) copy-start(bf16[1,144,48]{2,1,0:T(8,128)(2,1)} %copy-done.19) | copy-start | bytes 41476
  317.2 4.7 %copy-start.22 = (bf16[1,144,48]{2,1,0:T(8,128)(2,1)S(1)}, bf16[1,144,48]{2,1,0:T(8,128)(2,1)}, u32[]{:S(2)}) copy-start(bf16[1,144,48]{2,1,0:T(8,128)(2,1)} %copy-done.21) | copy-start | bytes 41476
  318.3 3.8 %copy-start.24 = (bf16[1,144,48]{2,1,0:T(8,128)(2,1)S(1)}, bf16[1,144,48]{2,1,0:T(8,128)(2,1)}, u32[]{:S(2)}) copy-start(bf16[1,144,48]{2,1,0:T(8,128)(2,1)} %copy-done.23) | copy-start | bytes 41476
  340.3 3.6 %copy-start.4 = (f32[2,14,14,144]{3,0,2,1:T(2,128)S(1)}, f32[2,14,14,144]{3,0,2,1:T(2,128)}, u32[]{:S(2)}) copy-start(f32[2,14,14,144]{3,0,2,1:T(2,128)} %reshape.201) | copy-start | bytes 677380
  342.1 3.3 copy-start.5
  342.5 2.9 copy-start.6
Sparse Core Ops, SparseCore 0:
  11.3 88.0 all-gather.7
  102.8 82.4 all-gather.5
  193.2 77.0 all-reduce.13
